TPU v7x, 512 devices: a whole 4x8x8 slice. The times are simulated.
512 devices in a mesh: stream: 32 (over y, z_lo), span: 16 (over x, z_hi, core).
Axes of the slice: x: 4, y: 8, z: 8 (z_hi: 2, z_lo: 4; z = z_hi * 4 + z_lo), core: 2. Of those that a mesh axis runs over, the one named last changes fastest.
Arguments:
- right_sides: bfloat16 [32, 16, 4, 512, 128], P('stream', 'span'), may hold values from -2.5 to 2.5
- inverse: bfloat16 [32, 16, 4, 512, 512], P('stream', 'span'), as said below
- coupling: bfloat16 [32, 16, 4, 3, 64, 512], P('stream', 'span')
- sweep_order: int32 [32, 16, 4], P('stream', 'span'), may hold values from 0 to 3, each once within a row
Outputs:
- solution: bfloat16 [32, 16, 4, 512, 128], P('stream', 'span')
Inputs may be any that keep to these rules, and one draw needn't show every extreme that they name: `sweep_order`: each group's 4 slots appear once each. Every diagonal block's inverse is well conditioned and of order one.
All inputs are finite; a program needn't handle non-finite values.
Results may differ from a plain program's by a relative error of at most 0.024.
Values may be sent and summed in bfloat16 or wider, within the bound.
A program may use at most 64 MiB of HBM per device.

v0:
```python
import jax
import jax.numpy as jnp
from jax import lax
from jax.experimental import pallas as pl
from jax.experimental.pallas import tpu as pltpu
from jax.sharding import PartitionSpec as P

SWEEPS = 6
EL = 4
NODES = 512
FACE = 64
RHS = 128
ROW = 4
F32 = jnp.float32
BF16 = jnp.bfloat16
MESH = pl.DeviceIdType.MESH


def mm(left, right):
    return jnp.dot(left, right, preferred_element_type=F32)


def mm_nt(left, right):
    return lax.dot_general(left, right, (((1,), (1,)), ((), ())), preferred_element_type=F32)


def split(value):
    high = value.astype(BF16)
    return high, (value - high.astype(F32)).astype(BF16)


def left_pair(value):
    return jnp.concatenate(split(value), axis=1)


def twice(value):
    return jnp.concatenate([value, value], axis=0)


def mm_fine(pair, right):
    high, low = split(right)
    return mm(
        jnp.concatenate([pair, pair[:, :FACE]], axis=1),
        jnp.concatenate([high, high, low], axis=0),
    )


def faces_of(values):
    lower = [values[64 * a : 64 * a + 8] for a in range(8)]
    upper = [values[64 * a + 56 : 64 * a + 64] for a in range(8)]
    return jnp.concatenate([values[NODES - FACE :]] + lower + upper, axis=0)


def kernel(
    rows, spans,
    order_ref, rs_hbm, inv_hbm, cpl_hbm,
    out_hbm,
    rs, inv, cpl, out_v,
    lift_full, side_full, gain_full, lift_face, side_face, gain_face,
    o_mat, f_mat, fe_mat, o_const, f_const, s_mat, se_mat, s_const,
    step_mats, inflow,
    xbuf, ysend, offbuf, tbuf, cin, csend, pre, pre_out,
    in_sem, out_sem, row_s, row_r, t_s, t_r, c_s, c_r, face_s, face_r,
):
    g = lax.axis_index("stream")
    s = lax.axis_index("span")
    y = g // ROW
    z = g % ROW

    def in_copies(t):
        return [
            pltpu.make_async_copy(inv_hbm.at[t], inv.at[t], in_sem.at[t, 0]),
            pltpu.make_async_copy(cpl_hbm.at[t], cpl.at[t], in_sem.at[t, 1]),
            pltpu.make_async_copy(rs_hbm.at[t], rs.at[t], in_sem.at[t, 2]),
        ]

    for t in range(EL):
        for c in in_copies(t):
            c.start()

    has_up = y > 0
    has_down = y < rows - 1
    has_below = s > 0
    has_above = s < spans - 1

    barrier = pltpu.get_barrier_semaphore()

    def greet(a, b):
        pl.semaphore_signal(barrier, inc=1, device_id=(a, b), device_id_type=MESH)

    for j in range(1, ROW):
        greet(y * ROW + (z + j) % ROW, s)
    pl.when(has_up)(lambda: greet(g - ROW, s))
    pl.when(has_down)(lambda: greet(g + ROW, s))
    pl.when(has_below)(lambda: greet(g, s - 1))
    pl.when(has_above)(lambda: greet(g, s + 1))

    xbuf[0] = jnp.zeros((2, EL, FACE, RHS), BF16)

    @pl.when(jnp.logical_not(has_below))
    def _():
        for k in range(1, SWEEPS):
            xbuf[k, 0] = jnp.zeros((EL, FACE, RHS), BF16)

    @pl.when(jnp.logical_not(has_above))
    def _():
        for k in range(1, SWEEPS):
            xbuf[k, 1] = jnp.zeros((EL, FACE, RHS), BF16)

    @pl.when(jnp.logical_not(has_up))
    def _():
        cin[...] = jnp.zeros(cin.shape, BF16)

    for t in range(EL):
        for c in in_copies(t):
            c.wait()
        maps = mm_nt(inv[t], cpl[t])
        gains = mm(inv[t], rs[t])
        lift_full[t] = left_pair(maps[:, :FACE])
        side_full[t] = maps[:, FACE:].astype(BF16)
        gain_full[t] = gains
        chosen = faces_of(maps)
        lift_face[t] = left_pair(chosen[:, :FACE])
        side_face[t] = chosen[:, FACE:]
        gain_face[t] = faces_of(gains)

    slots = [order_ref[p] for p in range(EL)]
    blocks = None
    f_mat[...] = jnp.zeros(f_mat.shape, BF16)
    s_mat[...] = jnp.zeros(s_mat.shape, BF16)
    for p in range(EL):
        lift = lift_face[slots[p]]
        side = side_face[slots[p]]
        gain = gain_face[slots[p]]
        if p == 0:
            lift_own = lift[:, :FACE].astype(F32) + lift[:, FACE:].astype(F32)
            result = jnp.concatenate([side, gain, lift_own], axis=1)
        else:
            moved = mm_fine(lift, blocks)
            result = jnp.concatenate(
                [moved[:, : 128 * p], side, moved[:, 128 * p : 128 * p + 128] + gain, moved[:, 128 * p + 128 :]],
                axis=1,
            )
        wide = 128 * (p + 1)
        for layer in range(2):
            at = layer * EL * FACE + p * FACE
            part = result[FACE + layer * FACE : 2 * FACE + layer * FACE]
            f_mat[at : at + FACE, :wide] = part[:, :wide].astype(BF16)
            f_const[at : at + FACE] = part[:, wide : wide + 128]
            fe_mat[at : at + FACE] = left_pair(part[:, wide + 128 :])
        blocks = result[:FACE]
        if p < EL - 1:
            s_mat[p * FACE : p * FACE + FACE, :wide] = blocks[:, :wide].astype(BF16)
            s_const[p * FACE : p * FACE + FACE] = blocks[:, wide : wide + 128]
            se_mat[p * FACE : p * FACE + FACE] = left_pair(blocks[:, wide + 128 :])
    o_mat[...] = blocks[:, :512].astype(BF16)
    o_const[...] = blocks[:, 512:640]
    tbuf[z] = left_pair(blocks[:, 640:])
    offbuf[0, z] = blocks[:, 512:640].astype(BF16)

    greetings = (
        ROW - 1
        + has_up.astype(jnp.int32)
        + has_down.astype(jnp.int32)
        + has_below.astype(jnp.int32)
        + has_above.astype(jnp.int32)
    )
    pl.semaphore_wait(barrier, greetings)

    def map_copy(j, who):
        return pltpu.make_async_remote_copy(
            tbuf.at[who], tbuf.at[who], t_s.at[j - 1], t_r.at[j - 1],
            device_id=(y * ROW + (z + j) % ROW, s), device_id_type=MESH,
        )

    def row_copy(k, j, who):
        return pltpu.make_async_remote_copy(
            offbuf.at[k, who], offbuf.at[k, who], row_s.at[k, j - 1], row_r.at[k, j - 1],
            device_id=(y * ROW + (z + j) % ROW, s), device_id_type=MESH,
        )

    def carry_copy(k):
        return pltpu.make_async_remote_copy(
            csend.at[k], cin.at[k], c_s.at[k], c_r.at[k],
            device_id=(g + ROW, s), device_id_type=MESH,
        )

    def face_copy(k, layer):
        return pltpu.make_async_remote_copy(
            ysend.at[k, layer], xbuf.at[k + 1, 1 - layer], face_s.at[k, layer], face_r.at[k, layer],
            device_id=(g, s - 1 if layer == 0 else s + 1), device_id_type=MESH,
        )

    def stacked(k):
        return jnp.concatenate(
            [xbuf[k, side, p] for p in range(EL) for side in range(2)], axis=0
        )

    for j in range(1, ROW):
        map_copy(j, z).start()
    for j in range(1, ROW):
        row_copy(0, j, z).start()

    for j in range(1, ROW):
        map_copy(j, (z + ROW - j) % ROW).wait_recv()
    state = None
    eye = (
        lax.broadcasted_iota(jnp.int32, (FACE, FACE), 0) == lax.broadcasted_iota(jnp.int32, (FACE, FACE), 1)
    ).astype(F32)
    none = jnp.zeros((FACE, FACE), F32)
    state = jnp.concatenate([none] * ROW + [eye], axis=1)
    for q in range(ROW + 1):
        step_mats[q] = jnp.concatenate(
            [left_pair(state[:, : ROW * FACE]), left_pair(state[:, ROW * FACE :])], axis=1
        )
        if q < ROW:
            state = mm_fine(tbuf[q], state) + jnp.concatenate(
                [eye if r == q else none for r in range(ROW)] + [none], axis=1
            )

    def row_stage(k):
        for j in range(1, ROW):
            row_copy(k, j, (z + ROW - j) % ROW).wait_recv()
        offsets = jnp.concatenate([offbuf[k, q] for q in range(ROW)], axis=0)
        both = jnp.concatenate([step_mats[ROW], step_mats[z]], axis=0)
        local = mm(both[:, : 2 * ROW * FACE], twice(offsets))

        @pl.when(has_up)
        def _():
            carry_copy(k).wait_recv()

        full = local + mm(both[:, 2 * ROW * FACE :], twice(cin[k]))

        @pl.when(has_down)
        def _():
            csend[k] = full[:FACE].astype(BF16)
            carry_copy(k).start()

        return full[FACE:].astype(BF16)

    @pl.loop(0, SWEEPS - 1)
    def _(k):
        pre[...] = mm(f_mat[...], stacked(k)) + f_const[...]
        entry = row_stage(k)
        faces = (pre[...] + mm(fe_mat[...], twice(entry))).astype(BF16)
        for layer in range(2):
            for p in range(EL):
                at = layer * EL * FACE + p * FACE
                ysend[k, layer, p] = faces[at : at + FACE]

        @pl.when(has_below)
        def _():
            face_copy(k, 0).start()

        @pl.when(has_above)
        def _():
            face_copy(k, 1).start()

        @pl.when(has_above)
        def _():
            face_copy(k, 0).wait_recv()

        @pl.when(has_below)
        def _():
            face_copy(k, 1).wait_recv()

        offbuf[k + 1, z] = (mm(o_mat[...], stacked(k + 1)) + o_const[...]).astype(BF16)
        for j in range(1, ROW):
            row_copy(k + 1, j, z).start()

    last = SWEEPS - 1
    places = []
    for t in range(EL):
        place = jnp.int32(0)
        for p in range(1, EL):
            place = jnp.where(slots[p] == t, p, place)
        places.append(place)
    traces = mm(s_mat[...], stacked(last)) + s_const[...]
    for t in range(EL):
        sides = jnp.concatenate([xbuf[last, 0, places[t]], xbuf[last, 1, places[t]]], axis=0)
        pre_out[t] = gain_full[t] + mm(side_full[t], sides)
    entry = row_stage(last)
    traces = (traces + mm(se_mat[...], twice(entry))).astype(BF16)
    inflow[0] = entry
    for p in range(1, EL):
        inflow[p] = traces[(p - 1) * FACE : p * FACE]

    def out_copy(t):
        return pltpu.make_async_copy(out_v.at[t], out_hbm.at[t], out_sem.at[t])

    for t in range(EL):
        out_v[t] = (pre_out[t] + mm(lift_full[t], twice(inflow[places[t]]))).astype(BF16)
        out_copy(t).start()

    for j in range(1, ROW):
        map_copy(j, z).wait_send()

    @pl.loop(0, SWEEPS)
    def _(k):
        for j in range(1, ROW):
            row_copy(k, j, z).wait_send()
        pl.when(has_down)(lambda: carry_copy(k).wait_send())

    @pl.loop(0, SWEEPS - 1)
    def _(k):
        pl.when(has_below)(lambda: face_copy(k, 0).wait_send())
        pl.when(has_above)(lambda: face_copy(k, 1).wait_send())

    for t in range(EL):
        out_copy(t).wait()


def shards(rows, spans, right_sides, inverse, coupling, sweep_order):
    vmem = pltpu.VMEM
    dma = pltpu.SemaphoreType.DMA
    any_space = pl.BlockSpec(memory_space=pltpu.HBM)
    placed = pl.pallas_call(
        lambda *refs: kernel(rows, spans, *refs),
        name="sweeps",
        out_shape=jax.ShapeDtypeStruct((EL, NODES, RHS), BF16),
        in_specs=[pl.BlockSpec(memory_space=pltpu.SMEM), any_space, any_space, any_space],
        out_specs=any_space,
        scratch_shapes=[
            vmem((EL, NODES, RHS), BF16),
            vmem((EL, NODES, NODES), BF16),
            vmem((EL, 3 * FACE, NODES), BF16),
            vmem((EL, NODES, RHS), BF16),
            vmem((EL, NODES, 2 * FACE), BF16),
            vmem((EL, NODES, 2 * FACE), BF16),
            vmem((EL, NODES, RHS), F32),
            vmem((EL, 3 * FACE, 2 * FACE), BF16),
            vmem((EL, 3 * FACE, 2 * FACE), F32),
            vmem((EL, 3 * FACE, RHS), F32),
            vmem((FACE, 512), BF16),
            vmem((512, 512), BF16),
            vmem((512, 2 * FACE), BF16),
            vmem((FACE, RHS), F32),
            vmem((512, RHS), F32),
            vmem((3 * FACE, 512), BF16),
            vmem((3 * FACE, 2 * FACE), BF16),
            vmem((3 * FACE, RHS), F32),
            vmem((ROW + 1, FACE, 2 * (ROW * FACE + FACE)), BF16),
            vmem((EL, FACE, RHS), BF16),
            vmem((SWEEPS, 2, EL, FACE, RHS), BF16),
            vmem((SWEEPS - 1, 2, EL, FACE, RHS), BF16),
            vmem((SWEEPS, ROW, FACE, RHS), BF16),
            vmem((ROW, FACE, 128), BF16),
            vmem((SWEEPS, FACE, RHS), BF16),
            vmem((SWEEPS, FACE, RHS), BF16),
            vmem((512, RHS), F32),
            vmem((EL, NODES, RHS), F32),
            dma((EL, 3)),
            dma((EL,)),
            dma((SWEEPS, ROW - 1)),
            dma((SWEEPS, ROW - 1)),
            dma((ROW - 1,)),
            dma((ROW - 1,)),
            dma((SWEEPS,)),
            dma((SWEEPS,)),
            dma((SWEEPS - 1, 2)),
            dma((SWEEPS - 1, 2)),
        ],
        compiler_params=pltpu.CompilerParams(
            collective_id=0, has_side_effects=True, vmem_limit_bytes=58 * 2**20
        ),
    )(
        sweep_order[0, 0],
        right_sides[0, 0],
        inverse[0, 0],
        coupling[0, 0].reshape(EL, 3 * FACE, NODES),
    )
    return placed[None, None]


def solution(mesh):
    rows = mesh.shape["stream"] // ROW
    spans = mesh.shape["span"]
    in_specs = (
        P("stream", "span", None, None, None),
        P("stream", "span", None, None, None),
        P("stream", "span", None, None, None, None),
        P("stream", "span", None),
    )
    out_specs = P("stream", "span", None, None, None)

    def run(right_sides, inverse, coupling, sweep_order):
        return shards(rows, spans, right_sides, inverse, coupling, sweep_order)

    return jax.shard_map(run, mesh=mesh, in_specs=in_specs, out_specs=out_specs, check_vma=False)
```

profile of v0, /device:TPU:59, one launch (start us, length us, event | category | flops | bytes accessed | tf_op | source)
XLA Modules:
  0.0 89.7 jit_solution(11326518512319226228)
XLA Ops:
  0.0 87.8 %sweeps.1 = bf16[4,512,128]{2,1,0:T(8,128)(2,1)} custom-call(s32[4]{0:T(128)} %bitcast.9, bf16[4,512,128]{2,1,0:T(8,128)(2,1)} %bitcast.8, bf16[4,512,512]{2,1,0:T(8,128)(2,1)} %bitcast.6, bf16[4,192,512]{2,1,0:T(8,128)(2,1)} %bitcast.7), custom_call_target="tpu_custom_call" | custom-call | tf_op jit(solution)/shard_map/sweeps/pallas_call | solution.py:317
  87.8 1.9 %copy.6 = bf16[1,1,4,512,128]{4,3,2,1,0:T(8,128)(2,1)} copy(bf16[1,1,4,512,128]{4,3,2,1,0:T(8,128)(2,1)} %bitcast.5) | data formatting | bytes 1048576
where the time goes:
time: 91 us; the launch traced here: 89.7 us
  Pallas kernels  87.8 us (96%)
  local copies, waits for them, and re-layouts  1.87 us (2%)
    pallas_call x1, Pallas kernels, shards(): pl.pallas_call(lambda *refs: kernel(rows, spans, *refs), name='sweeps', o...  87.8 us
    unnamed x1, local copies, waits for them, and re-layouts  1.87 us

commit v1 on v0

v1 whole, which is shorter than its diff:
```python
import jax
import jax.numpy as jnp
from jax import lax
from jax.experimental import pallas as pl
from jax.experimental.pallas import tpu as pltpu
from jax.sharding import PartitionSpec as P

SWEEPS = 6
EL = 4
NODES = 512
FACE = 64
RHS = 128
NB = 4
F32 = jnp.float32
BF16 = jnp.bfloat16
MESH = pl.DeviceIdType.MESH


def mm(left, right):
    return jnp.dot(left, right, preferred_element_type=F32)


def mm_nt(left, right):
    return lax.dot_general(left, right, (((1,), (1,)), ((), ())), preferred_element_type=F32)


def split(value):
    high = value.astype(BF16)
    return high, (value - high.astype(F32)).astype(BF16)


def left_pair(value):
    return jnp.concatenate(split(value), axis=1)


def twice(value):
    return jnp.concatenate([value, value], axis=0)


def mm_fine(pair, right):
    high, low = split(right)
    return mm(
        jnp.concatenate([pair, pair[:, :FACE]], axis=1),
        jnp.concatenate([high, high, low], axis=0),
    )


def faces_of(values):
    lower = [values[64 * a : 64 * a + 8] for a in range(8)]
    upper = [values[64 * a + 56 : 64 * a + 64] for a in range(8)]
    return jnp.concatenate([values[NODES - FACE :]] + lower + upper, axis=0)


def kernel(
    blocks_along, spans,
    order_ref, rs_hbm, inv_hbm, cpl_hbm,
    out_hbm,
    rs, inv, cpl, out_v,
    lift_full, side_full, gain_full, lift_face, side_face, gain_face,
    pf_mat, pf_const, fe_next, s_mat, se_mat, s_const,
    m_all, d_all, local, inflow, xs, pre_out,
    hsend, hbuf, msend, asend, mbuf, abuf, xbuf, ysend, ebuf, obuf, esend, pbuf, psend, cin, csend, efin,
    in_sem, out_sem, h_s, h_r, m_s, m_r, a_s, a_r,
    face_s, face_r, e_s, e_r, o_s, o_r, p_s, p_r, c_s, c_r, fin_s, fin_r,
):
    g = lax.axis_index("stream")
    s = lax.axis_index("span")
    block = g // NB
    m = g % NB

    odd = s % 2

    def owner_of(column):
        return block * NB + (NB - 1) * (column % 2), column - column % 2 + 1

    first_place = (m == 0).astype(jnp.int32)
    is_owner = jnp.logical_and(odd == 1, jnp.logical_or(m == 0, m == NB - 1))
    owned = s - first_place * odd
    owns_other = jnp.logical_and(is_owner, owned != s)
    owns_own = jnp.logical_and(is_owner, owned == s)
    has_up = block > 0
    has_down = block < blocks_along - 1
    has_side = (s > 0, s < spans - 1)
    owned_side = (owned > 0, owned < spans - 1)
    shift = (-1, 1)
    side_owner = (owner_of(s + 15), owner_of(s + 17))
    side_owner = tuple((a, b - 16) for a, b in side_owner)
    near_owner = tuple((a, b - 16) for a, b in (owner_of(owned + 15), owner_of(owned + 17)))
    own_owner = owner_of(s)
    to_self = (owns_other, jnp.bool_(False))

    def in_copies(t):
        return [
            pltpu.make_async_copy(inv_hbm.at[t], inv.at[t], in_sem.at[t, 0]),
            pltpu.make_async_copy(cpl_hbm.at[t], cpl.at[t], in_sem.at[t, 1]),
            pltpu.make_async_copy(rs_hbm.at[t], rs.at[t], in_sem.at[t, 2]),
        ]

    for t in range(EL):
        for c in in_copies(t):
            c.start()

    barrier = pltpu.get_barrier_semaphore()

    def greet(a, b):
        pl.semaphore_signal(barrier, inc=1, device_id=(a, b), device_id_type=MESH)

    def both(a, b):
        return jnp.logical_and(a, b)

    not_owner = jnp.logical_not(is_owner)
    not_own = jnp.logical_not(owns_own)
    for side in range(2):
        @pl.when(has_side[side])
        def _():
            greet(g, s + shift[side])

            @pl.when(jnp.logical_not(to_self[side]))
            def _():
                greet(*side_owner[side])

        @pl.when(both(is_owner, owned_side[side]))
        def _():
            greet(*near_owner[side])
            for q in range(NB):
                @pl.when(jnp.logical_not(both(owned + shift[side] == s, m == q)))
                def _():
                    greet(block * NB + q, owned + shift[side])

        @pl.when(jnp.logical_not(has_side[side]))
        def _():
            hbuf[side] = jnp.zeros((256, 128), BF16)
            for k in range(SWEEPS - 1):
                xbuf[k, side] = jnp.zeros((EL, FACE, RHS), BF16)
                ebuf[k, side] = jnp.zeros((FACE, RHS), BF16)

        @pl.when(both(is_owner, jnp.logical_not(owned_side[side])))
        def _():
            for k in range(SWEEPS - 1):
                obuf[k, side] = jnp.zeros((NB, FACE, RHS), BF16)
                pbuf[k, side] = jnp.zeros((NB, FACE, RHS), BF16)

    @pl.when(is_owner)
    def _():
        for q in range(NB):
            pl.when(jnp.logical_not(both(owned == s, m == q)))(lambda: greet(block * NB + q, owned))
        pl.when(has_up)(lambda: greet(g - NB, s))
        pl.when(has_down)(lambda: greet(g + NB, s))

    pl.when(not_own)(lambda: greet(*own_owner))

    @pl.when(jnp.logical_not(has_up))
    def _():
        cin[...] = jnp.zeros(cin.shape, BF16)

    for t in range(EL):
        for c in in_copies(t):
            c.wait()
        maps = mm_nt(inv[t], cpl[t])
        gains = mm(inv[t], rs[t])
        lift_full[t] = left_pair(maps[:, :FACE])
        side_full[t] = maps[:, FACE:].astype(BF16)
        gain_full[t] = gains
        chosen = faces_of(maps)
        lift_face[t] = left_pair(chosen[:, :FACE])
        side_face[t] = chosen[:, FACE:]
        gain_face[t] = faces_of(gains)

    slots = [order_ref[p] for p in range(EL)]
    trace = None
    pf_mat[...] = jnp.zeros(pf_mat.shape, BF16)
    s_mat[...] = jnp.zeros(s_mat.shape, BF16)
    face_entry = [[None] * EL, [None] * EL]
    for p in range(EL):
        lift = lift_face[slots[p]]
        side = side_face[slots[p]]
        gain = gain_face[slots[p]]
        if p == 0:
            lift_own = lift[:, :FACE].astype(F32) + lift[:, FACE:].astype(F32)
            result = jnp.concatenate([side, gain, lift_own], axis=1)
        else:
            moved = mm_fine(lift, trace)
            result = jnp.concatenate(
                [moved[:, : 128 * p], side, moved[:, 128 * p : 128 * p + 128] + gain, moved[:, 128 * p + 128 :]],
                axis=1,
            )
        wide = 128 * (p + 1)
        for layer in range(2):
            at = 128 + layer * EL * FACE + p * FACE
            part = result[FACE + layer * FACE : 2 * FACE + layer * FACE]
            pf_mat[at : at + FACE, :wide] = part[:, :wide].astype(BF16)
            pf_const[at : at + FACE] = part[:, wide : wide + 128]
            face_entry[layer][p] = part[:, wide + 128 :].astype(BF16)
            ysend[0, layer, p] = part[:, wide : wide + 128].astype(BF16)
        trace = result[:FACE]
        if p < EL - 1:
            s_mat[p * FACE : p * FACE + FACE, :wide] = trace[:, :wide].astype(BF16)
            s_const[p * FACE : p * FACE + FACE] = trace[:, wide : wide + 128]
            se_mat[p * FACE : p * FACE + FACE] = left_pair(trace[:, wide + 128 :])
    own_o = [
        jnp.concatenate([trace[:, 128 * p + 64 * side : 128 * p + 64 * side + 64] for p in range(EL)], axis=1).astype(BF16)
        for side in range(2)
    ]
    for side in range(2):
        fe = face_entry[side]
        hsend[side, :64] = own_o[side][:, :128]
        hsend[side, 64:128] = own_o[side][:, 128:]
        hsend[side, 128:] = jnp.concatenate(
            [jnp.concatenate([fe[0], fe[1]], axis=0), jnp.concatenate([fe[2], fe[3]], axis=0)], axis=1
        )
    msend[:64] = left_pair(trace[:, 640:])
    msend[64:] = trace[:, 512:640].astype(BF16)

    @pl.when(owns_own)
    def _():
        mbuf[m] = msend[...]

    def number(flag):
        return flag.astype(jnp.int32)

    greetings = 2 * (number(has_side[0]) + number(has_side[1])) - number(owns_other) + number(not_own)
    greetings = greetings + number(is_owner) * (
        (NB + 1) * (number(owned_side[0]) + number(owned_side[1]))
        + NB + number(has_up) + number(has_down)
    ) - number(owns_other) - number(owns_own)
    pl.semaphore_wait(barrier, greetings)

    def remote(src, dst, send, recv, a, b):
        return pltpu.make_async_remote_copy(src, dst, send, recv, device_id=(a, b), device_id_type=MESH)

    def h_copy(side):
        return remote(hsend.at[side], hbuf.at[1 - side], h_s.at[side], h_r.at[1 - side], g, s + shift[side])

    def h_arrival(side):
        return remote(hsend.at[side], hbuf.at[side], h_s.at[side], h_r.at[side], g, s + shift[side])

    def map_copy(who):
        return remote(msend, mbuf.at[who], m_s, m_r.at[who], *own_owner)

    def a_copy(who):
        return remote(asend, abuf.at[who], a_s, a_r.at[who], *own_owner)

    def face_copy(k, side):
        return remote(
            ysend.at[k, side], xbuf.at[k, 1 - side], face_s.at[k, side], face_r.at[k, 1 - side], g, s + shift[side]
        )

    def face_arrival(k, side):
        return remote(ysend.at[k, side], xbuf.at[k, side], face_s.at[k, side], face_r.at[k, side], g, s + shift[side])

    def p_copy(k, side):
        return remote(
            psend.at[k, side], pbuf.at[k, 1 - side, m], p_s.at[k, side], p_r.at[k, 1 - side],
            *side_owner[side],
        )

    def p_local(k, side):
        return pltpu.make_async_copy(psend.at[k, side], pbuf.at[k, 1 - side, m], p_r.at[k, 1 - side])

    def p_start(k, side):
        pl.when(both(has_side[side], jnp.logical_not(to_self[side])))(lambda: p_copy(k, side).start())
        pl.when(both(has_side[side], to_self[side]))(lambda: p_local(k, side).start())

    def p_arrival(k, side):
        return remote(pbuf.at[k, side], pbuf.at[k, side], p_s.at[k, side], p_r.at[k, side], g, s + shift[side])

    def owner_copy(k, side):
        return remote(
            esend.at[k], obuf.at[k, 1 - side], o_s.at[k, side], o_r.at[k, 1 - side], *near_owner[side]
        )

    def owner_arrival(k, side):
        return remote(esend.at[k], obuf.at[k, side], o_s.at[k, side], o_r.at[k, side], g, s + shift[side])

    def entry_copy(k, side, q):
        return remote(
            esend.at[k, q], ebuf.at[k, 1 - side], e_s.at[k, side, q], e_r.at[k, 1 - side],
            block * NB + q, owned + shift[side],
        )

    def entry_local(k, side, q):
        return pltpu.make_async_copy(esend.at[k, q], ebuf.at[k, 1 - side], e_r.at[k, 1 - side])

    def entry_self(side, q):
        return both(owned + shift[side] == s, m == q)

    def entry_arrival(k, side):
        return remote(esend.at[k, 0], ebuf.at[k, side], e_s.at[k, side], e_r.at[k, side], g, s + shift[side])

    def carry_copy(k):
        return remote(csend.at[k], cin.at[k], c_s.at[k], c_r.at[k], g + NB, s)

    def last_copy(q):
        return remote(esend.at[SWEEPS - 1, q], efin, fin_s.at[q], fin_r, block * NB + q, owned)

    pl.when(not_own)(lambda: map_copy(m).start())
    for side in range(2):
        pl.when(has_side[side])(lambda: h_copy(side).start())
    for side in range(2):
        pl.when(has_side[side])(lambda: face_copy(0, side).start())

    def owner_finish(k, final):
        pl.when(has_up)(lambda: carry_copy(k).wait_recv())
        carried = twice(cin[k])
        out = local[NB * FACE :] + mm(d_all[NB * FACE :], carried)

        @pl.when(has_down)
        def _():
            csend[k] = out.astype(BF16)
            carry_copy(k).start()

        entries = (local[: NB * FACE] + mm(d_all[: NB * FACE], carried)).astype(BF16)
        for q in range(NB):
            esend[k, q] = entries[q * FACE : q * FACE + FACE]
        if final:
            for q in range(NB):
                pl.when(jnp.logical_not(both(owned == s, m == q)))(lambda: last_copy(q).start())

            @pl.when(owns_own)
            def _():
                efin[...] = esend[k, m]
        else:
            for side in range(2):
                @pl.when(owned_side[side])
                def _():
                    for q in range(NB):
                        pl.when(jnp.logical_not(entry_self(side, q)))(lambda: entry_copy(k, side, q).start())
                        pl.when(entry_self(side, q))(lambda: entry_local(k, side, q).start())
            for side in range(2):
                pl.when(owned_side[side])(lambda: owner_copy(k, side).start())

    @pl.when(is_owner)
    def _():
        for q in range(NB):
            pl.when(jnp.logical_not(both(owned == s, m == q)))(lambda: map_copy(q).wait_recv())
        eye = (
            lax.broadcasted_iota(jnp.int32, (FACE, FACE), 0) == lax.broadcasted_iota(jnp.int32, (FACE, FACE), 1)
        ).astype(F32)
        none = jnp.zeros((FACE, FACE), F32)
        state = jnp.concatenate([none] * NB + [eye], axis=1)
        for q in range(NB + 1):
            m_all[q * FACE : q * FACE + FACE] = left_pair(state[:, : NB * FACE])
            d_all[q * FACE : q * FACE + FACE] = left_pair(state[:, NB * FACE :])
            if q < NB:
                state = mm_fine(mbuf[q, :64], state) + jnp.concatenate(
                    [eye if r == q else none for r in range(NB)] + [none], axis=1
                )
        starts = jnp.concatenate([mbuf[q, 64:] for q in range(NB)], axis=0)
        local[...] = mm(m_all[...], twice(starts))
        pl.when(jnp.logical_not(has_up))(lambda: owner_finish(0, False))

    for side in range(2):
        pl.when(has_side[side])(lambda: h_arrival(side).wait_recv())
    from_o = [jnp.concatenate([hbuf[side, :64], hbuf[side, 64:128]], axis=1) for side in range(2)]
    from_fe = [jnp.concatenate([hbuf[side, 128:, :64], hbuf[side, 128:, 64:]], axis=0) for side in range(2)]
    for side in range(2):
        at = 128 + side * EL * FACE
        pf_const[64 * side : 64 * side + 64] = mm(from_o[side], pf_const[at : at + 256].astype(BF16))
        psend[0, side] = pf_const[64 * side : 64 * side + 64].astype(BF16)
        p_start(0, side)
    asend[...] = jnp.concatenate([mm(own_o[side], from_fe[side]) for side in range(2)], axis=1).astype(BF16)
    pl.when(not_own)(lambda: a_copy(m).start())

    @pl.when(owns_own)
    def _():
        abuf[m] = asend[...]

    blank = jnp.zeros((FACE, FACE), BF16)
    for side in range(2):
        at = 128 + side * EL * FACE
        pf_mat[64 * side : 64 * side + 64] = mm(from_o[side], pf_mat[at : at + 256]).astype(BF16)
        for p in range(EL):
            part = from_fe[side][p * FACE : p * FACE + FACE]
            row = 128 * p + 64 * side
            fe_next[row : row + FACE] = jnp.concatenate([part, blank] if side == 0 else [blank, part], axis=1)

    @pl.when(is_owner)
    def _():
        pl.when(has_up)(lambda: owner_finish(0, False))
        for q in range(NB):
            pl.when(jnp.logical_not(both(owned == s, m == q)))(lambda: a_copy(q).wait_recv())

    def owner_gather(k):
        for side in range(2):
            @pl.when(owned_side[side])
            def _():
                p_arrival(k, side).wait_recv()
                owner_arrival(k, side).wait_recv()
        offsets = []
        for q in range(NB):
            known = mbuf[q, 64:].astype(F32) + pbuf[k, 0, q].astype(F32) + pbuf[k, 1, q].astype(F32)
            coming = jnp.concatenate([obuf[k, 0, q], obuf[k, 1, q]], axis=0)
            offsets.append((known + mm(abuf[q], coming)).astype(BF16))
        local[...] = mm(m_all[...], twice(jnp.concatenate(offsets, axis=0)))

    def member_gather(k):
        for side in range(2):
            @pl.when(has_side[side])
            def _():
                entry_arrival(k, side).wait_recv()
                face_arrival(k, side).wait_recv()
        early = jnp.concatenate([xbuf[k, side, p] for p in range(EL) for side in range(2)], axis=0)
        entries = jnp.concatenate([ebuf[k, 0], ebuf[k, 1]], axis=0)
        now = (early.astype(F32) + mm(fe_next[...], entries)).astype(BF16)
        for p in range(EL):
            xs[p] = now[128 * p : 128 * p + 128]
        return now

    @pl.loop(0, SWEEPS - 2)
    def _(k):
        now = member_gather(k)
        for side in range(2):
            at = 128 + side * EL * FACE
            ahead = (mm(pf_mat[at : at + 256], now) + pf_const[at : at + 256]).astype(BF16)
            for p in range(EL):
                ysend[k + 1, side, p] = ahead[p * FACE : p * FACE + FACE]
            pl.when(has_side[side])(lambda: face_copy(k + 1, side).start())
        ahead = (mm(pf_mat[:128], now) + pf_const[:128]).astype(BF16)
        for side in range(2):
            psend[k + 1, side] = ahead[64 * side : 64 * side + 64]
            p_start(k + 1, side)
        @pl.when(is_owner)
        def _():
            owner_gather(k)
            owner_finish(k + 1, False)

    last = SWEEPS - 1

    @pl.when(is_owner)
    def _():
        owner_gather(last - 1)
        owner_finish(last, True)

    now = member_gather(last - 1)
    places = []
    for t in range(EL):
        place = jnp.int32(0)
        for p in range(1, EL):
            place = jnp.where(slots[p] == t, p, place)
        places.append(place)
    traces = mm(s_mat[...], now) + s_const[...]
    for t in range(EL):
        pre_out[t] = gain_full[t] + mm(side_full[t], xs[places[t]])
    pl.when(not_own)(lambda: last_copy(m).wait_recv())
    entry = efin[...]
    traces = (traces + mm(se_mat[...], twice(entry))).astype(BF16)
    inflow[0] = entry
    for p in range(1, EL):
        inflow[p] = traces[(p - 1) * FACE : p * FACE]

    def out_copy(t):
        return pltpu.make_async_copy(out_v.at[t], out_hbm.at[t], out_sem.at[t])

    for t in range(EL):
        out_v[t] = (pre_out[t] + mm(lift_full[t], twice(inflow[places[t]]))).astype(BF16)
        out_copy(t).start()

    @pl.when(not_own)
    def _():
        map_copy(m).wait_send()
        a_copy(m).wait_send()

    for side in range(2):
        pl.when(has_side[side])(lambda: h_copy(side).wait_send())

    @pl.loop(0, SWEEPS - 1)
    def _(k):
        for side in range(2):
            pl.when(has_side[side])(lambda: face_copy(k, side).wait_send())
            pl.when(both(has_side[side], jnp.logical_not(to_self[side])))(lambda: p_copy(k, side).wait_send())

            @pl.when(both(is_owner, owned_side[side]))
            def _():
                owner_copy(k, side).wait_send()
                for q in range(NB):
                    pl.when(jnp.logical_not(entry_self(side, q)))(lambda: entry_copy(k, side, q).wait_send())

    @pl.when(is_owner)
    def _():
        @pl.when(has_down)
        def _():
            @pl.loop(0, SWEEPS)
            def _(k):
                carry_copy(k).wait_send()

        for q in range(NB):
            pl.when(jnp.logical_not(both(owned == s, m == q)))(lambda: last_copy(q).wait_send())

    for t in range(EL):
        out_copy(t).wait()


def shards(blocks_along, spans, right_sides, inverse, coupling, sweep_order):
    vmem = pltpu.VMEM
    dma = pltpu.SemaphoreType.DMA
    hbm = pl.BlockSpec(memory_space=pltpu.HBM)
    trips = SWEEPS - 1
    placed = pl.pallas_call(
        lambda *refs: kernel(blocks_along, spans, *refs),
        name="sweeps",
        out_shape=jax.ShapeDtypeStruct((EL, NODES, RHS), BF16),
        in_specs=[pl.BlockSpec(memory_space=pltpu.SMEM), hbm, hbm, hbm],
        out_specs=hbm,
        scratch_shapes=[
            vmem((EL, NODES, RHS), BF16),
            vmem((EL, NODES, NODES), BF16),
            vmem((EL, 3 * FACE, NODES), BF16),
            vmem((EL, NODES, RHS), BF16),
            vmem((EL, NODES, 2 * FACE), BF16),
            vmem((EL, NODES, 2 * FACE), BF16),
            vmem((EL, NODES, RHS), F32),
            vmem((EL, 3 * FACE, 2 * FACE), BF16),
            vmem((EL, 3 * FACE, 2 * FACE), F32),
            vmem((EL, 3 * FACE, RHS), F32),
            vmem((640, 512), BF16),
            vmem((640, RHS), F32),
            vmem((512, 128), BF16),
            vmem((3 * FACE, 512), BF16),
            vmem((3 * FACE, 2 * FACE), BF16),
            vmem((3 * FACE, RHS), F32),
            vmem(((NB + 1) * FACE, 2 * NB * FACE), BF16),
            vmem(((NB + 1) * FACE, 2 * FACE), BF16),
            vmem(((NB + 1) * FACE, RHS), F32),
            vmem((EL, FACE, RHS), BF16),
            vmem((EL, 2 * FACE, RHS), BF16),
            vmem((EL, NODES, RHS), F32),
            vmem((2, 256, 128), BF16),
            vmem((2, 256, 128), BF16),
            vmem((128, 128), BF16),
            vmem((FACE, 128), BF16),
            vmem((NB, 128, 128), BF16),
            vmem((NB, FACE, 128), BF16),
            vmem((trips, 2, EL, FACE, RHS), BF16),
            vmem((trips, 2, EL, FACE, RHS), BF16),
            vmem((trips, 2, FACE, RHS), BF16),
            vmem((trips, 2, NB, FACE, RHS), BF16),
            vmem((SWEEPS, NB, FACE, RHS), BF16),
            vmem((trips, 2, NB, FACE, RHS), BF16),
            vmem((trips, 2, FACE, RHS), BF16),
            vmem((SWEEPS, FACE, RHS), BF16),
            vmem((SWEEPS, FACE, RHS), BF16),
            vmem((FACE, RHS), BF16),
            dma((EL, 3)),
            dma((EL,)),
            dma((2,)),
            dma((2,)),
            dma,
            dma((NB,)),
            dma,
            dma((NB,)),
            dma((trips, 2)),
            dma((trips, 2)),
            dma((trips, 2, NB)),
            dma((trips, 2)),
            dma((trips, 2)),
            dma((trips, 2)),
            dma((trips, 2)),
            dma((trips, 2)),
            dma((SWEEPS,)),
            dma((SWEEPS,)),
            dma((NB,)),
            dma,
        ],
        compiler_params=pltpu.CompilerParams(
            collective_id=0, has_side_effects=True, vmem_limit_bytes=58 * 2**20
        ),
    )(
        sweep_order[0, 0],
        right_sides[0, 0],
        inverse[0, 0],
        coupling[0, 0].reshape(EL, 3 * FACE, NODES),
    )
    return placed[None, None]


def solution(mesh):
    blocks_along = mesh.shape["stream"] // NB
    spans = mesh.shape["span"]
    in_specs = (
        P("stream", "span", None, None, None),
        P("stream", "span", None, None, None),
        P("stream", "span", None, None, None, None),
        P("stream", "span", None),
    )
    out_specs = P("stream", "span", None, None, None)

    def run(right_sides, inverse, coupling, sweep_order):
        return shards(blocks_along, spans, right_sides, inverse, coupling, sweep_order)

    return jax.shard_map(run, mesh=mesh, in_specs=in_specs, out_specs=out_specs, check_vma=False)
```

time: 91 us -> 80.2 us (0.88)
  the two profiles are of different devices: /device:TPU:59 before, /device:TPU:61 now
where the time goes in v1:
time: 80.2 us; the launch traced here: 80.1 us
  Pallas kernels  78.2 us (98%)
  local copies, waits for them, and re-layouts  1.87 us (2%)
    pallas_call x1, Pallas kernels, shards(): pl.pallas_call(lambda *refs: kernel(blocks_along, spans, *refs), name='sw...  78.2 us
    unnamed x1, local copies, waits for them, and re-layouts  1.87 us

profile of v1, /device:TPU:61, one launch (start us, length us, event | category | flops | bytes accessed | tf_op | source)
XLA Modules:
  0.0 80.1 jit_solution(16737568392979335946)
XLA Ops:
  0.0 78.2 %sweeps.1 = bf16[4,512,128]{2,1,0:T(8,128)(2,1)} custom-call(s32[4]{0:T(128)} %bitcast.9, bf16[4,512,128]{2,1,0:T(8,128)(2,1)} %bitcast.8, bf16[4,512,512]{2,1,0:T(8,128)(2,1)} %bitcast.6, bf16[4,192,512]{2,1,0:T(8,128)(2,1)} %bitcast.7), custom_call_target="tpu_custom_call" | custom-call | tf_op jit(solution)/shard_map/sweeps/pallas_call | solution.py:498
  78.2 1.9 %copy.6 = bf16[1,1,4,512,128]{4,3,2,1,0:T(8,128)(2,1)} copy(bf16[1,1,4,512,128]{4,3,2,1,0:T(8,128)(2,1)} %bitcast.5) | data formatting | bytes 1048576

commit v2 on v1

--- a/solution.py
+++ b/solution.py
@@ -45,10 +45,16 @@
     )
 
 
+def face_groups(values):
+    lower = [values[64 * a : 64 * a + 16] for a in range(8)]
+    upper = [values[64 * a + 48 : 64 * a + 64] for a in range(8)]
+    return jnp.concatenate([values[NODES - FACE :]] + lower + upper, axis=0)
+
+
 def faces_of(values):
-    lower = [values[64 * a : 64 * a + 8] for a in range(8)]
-    upper = [values[64 * a + 56 : 64 * a + 64] for a in range(8)]
-    return jnp.concatenate([values[NODES - FACE :]] + lower + upper, axis=0)
+    lower = [values[64 + 16 * a : 64 + 16 * a + 8] for a in range(8)]
+    upper = [values[192 + 16 * a + 8 : 192 + 16 * a + 16] for a in range(8)]
+    return jnp.concatenate([values[:FACE]] + lower + upper, axis=0)
 
 
 def kernel(
@@ -59,9 +65,9 @@
     lift_full, side_full, gain_full, lift_face, side_face, gain_face,
     pf_mat, pf_const, fe_next, s_mat, se_mat, s_const,
     m_all, d_all, local, inflow, xs, pre_out,
-    hsend, hbuf, msend, asend, mbuf, abuf, xbuf, ysend, ebuf, obuf, esend, pbuf, psend, cin, csend, efin,
+    hsend, hbuf, msend, asend, mbuf, abuf, xbuf, ysend, ebuf, obuf, esend, pbuf, psend, cin, csend, tin, tsend, chain, running, efin,
     in_sem, out_sem, h_s, h_r, m_s, m_r, a_s, a_r,
-    face_s, face_r, e_s, e_r, o_s, o_r, p_s, p_r, c_s, c_r, fin_s, fin_r,
+    face_s, face_r, e_s, e_r, o_s, o_r, p_s, p_r, c_s, c_r, t_s, t_r, fin_s, fin_r,
 ):
     g = lax.axis_index("stream")
     s = lax.axis_index("span")
@@ -79,7 +85,6 @@
     owns_other = jnp.logical_and(is_owner, owned != s)
     owns_own = jnp.logical_and(is_owner, owned == s)
     has_up = block > 0
-    has_down = block < blocks_along - 1
     has_side = (s > 0, s < spans - 1)
     owned_side = (owned > 0, owned < spans - 1)
     shift = (-1, 1)
@@ -144,27 +149,28 @@
     def _():
         for q in range(NB):
             pl.when(jnp.logical_not(both(owned == s, m == q)))(lambda: greet(block * NB + q, owned))
-        pl.when(has_up)(lambda: greet(g - NB, s))
-        pl.when(has_down)(lambda: greet(g + NB, s))
+        for i in range(1, blocks_along):
+            greet((g + i * NB) % (blocks_along * NB), s)
 
     pl.when(not_own)(lambda: greet(*own_owner))
 
-    @pl.when(jnp.logical_not(has_up))
-    def _():
-        cin[...] = jnp.zeros(cin.shape, BF16)
+    before = blocks_along - 1
+    for j in range(before):
+        @pl.when(both(is_owner, j >= block))
+        def _():
+            chain[:, j * FACE : j * FACE + FACE] = jnp.zeros((FACE, FACE), BF16)
+            chain[:, (before + j) * FACE : (before + j) * FACE + FACE] = jnp.zeros((FACE, FACE), BF16)
+            for k in range(SWEEPS):
+                cin[k, j] = jnp.zeros((FACE, RHS), BF16)
 
     for t in range(EL):
         for c in in_copies(t):
             c.wait()
-        maps = mm_nt(inv[t], cpl[t])
-        gains = mm(inv[t], rs[t])
-        lift_full[t] = left_pair(maps[:, :FACE])
-        side_full[t] = maps[:, FACE:].astype(BF16)
-        gain_full[t] = gains
-        chosen = faces_of(maps)
+        rows = face_groups(inv[t])
+        chosen = faces_of(mm_nt(rows, cpl[t]))
         lift_face[t] = left_pair(chosen[:, :FACE])
         side_face[t] = chosen[:, FACE:]
-        gain_face[t] = faces_of(gains)
+        gain_face[t] = faces_of(mm(rows, rs[t]))
 
     slots = [order_ref[p] for p in range(EL)]
     trace = None
@@ -221,7 +227,7 @@
     greetings = 2 * (number(has_side[0]) + number(has_side[1])) - number(owns_other) + number(not_own)
     greetings = greetings + number(is_owner) * (
         (NB + 1) * (number(owned_side[0]) + number(owned_side[1]))
-        + NB + number(has_up) + number(has_down)
+        + NB + blocks_along - 1
     ) - number(owns_other) - number(owns_own)
     pl.semaphore_wait(barrier, greetings)
 
@@ -287,8 +293,50 @@
     def entry_arrival(k, side):
         return remote(esend.at[k, 0], ebuf.at[k, side], e_s.at[k, side], e_r.at[k, side], g, s + shift[side])
 
-    def carry_copy(k):
-        return remote(csend.at[k], cin.at[k], c_s.at[k], c_r.at[k], g + NB, s)
+    def rest_copy(k, ahead):
+        return remote(
+            csend.at[k], cin.at[k, block], c_s.at[k, ahead - 1], c_r.at[k, block], g + ahead * NB, s
+        )
+
+    def rest_arrival(k, j):
+        return remote(csend.at[k], cin.at[k, j], c_s.at[k, 0], c_r.at[k, j], g, s)
+
+    def turn_copy(ahead):
+        return remote(tsend, tin.at[block], t_s.at[ahead - 1], t_r.at[block], g + ahead * NB, s)
+
+    def turn_arrival(j):
+        return remote(tsend, tin.at[j], t_s.at[0], t_r.at[j], g, s)
+
+    def later(ahead):
+        return block + ahead < blocks_along
+
+    def send_rest(k):
+        csend[k] = local[NB * FACE :].astype(BF16)
+        for ahead in range(1, blocks_along):
+            pl.when(later(ahead))(lambda: rest_copy(k, ahead).start())
+
+    def form_chain():
+        eye = (
+            lax.broadcasted_iota(jnp.int32, (FACE, FACE), 0) == lax.broadcasted_iota(jnp.int32, (FACE, FACE), 1)
+        ).astype(F32)
+        for j in reversed(range(before)):
+            @pl.when(j + 1 == block)
+            def _():
+                running[...] = left_pair(eye)
+
+            if j + 1 < before:
+                @pl.when(j + 1 < block)
+                def _():
+                    turn_arrival(j + 1).wait_recv()
+                    turn = tin[j + 1, :, :FACE].astype(F32) + tin[j + 1, :, FACE:].astype(F32)
+                    running[...] = left_pair(mm_fine(running[...], turn))
+
+            @pl.when(j < block)
+            def _():
+                chain[:, j * FACE : j * FACE + FACE] = running[:, :FACE]
+                chain[:, (before + j) * FACE : (before + j) * FACE + FACE] = running[:, FACE:]
+
+        pl.when(has_up)(lambda: turn_arrival(0).wait_recv())
 
     def last_copy(q):
         return remote(esend.at[SWEEPS - 1, q], efin, fin_s.at[q], fin_r, block * NB + q, owned)
@@ -299,16 +347,17 @@
     for side in range(2):
         pl.when(has_side[side])(lambda: face_copy(0, side).start())
 
+    for t in range(EL):
+        maps = mm_nt(inv[t], cpl[t])
+        lift_full[t] = left_pair(maps[:, :FACE])
+        side_full[t] = maps[:, FACE:].astype(BF16)
+        gain_full[t] = mm(inv[t], rs[t])
+
     def owner_finish(k, final):
-        pl.when(has_up)(lambda: carry_copy(k).wait_recv())
-        carried = twice(cin[k])
-        out = local[NB * FACE :] + mm(d_all[NB * FACE :], carried)
-
-        @pl.when(has_down)
-        def _():
-            csend[k] = out.astype(BF16)
-            carry_copy(k).start()
-
+        for j in range(before):
+            pl.when(j < block)(lambda: rest_arrival(k, j).wait_recv())
+        rests = jnp.concatenate([cin[k, j] for j in range(before)], axis=0)
+        carried = twice(mm(chain[...], twice(rests)).astype(BF16))
         entries = (local[: NB * FACE] + mm(d_all[: NB * FACE], carried)).astype(BF16)
         for q in range(NB):
             esend[k, q] = entries[q * FACE : q * FACE + FACE]
@@ -345,8 +394,12 @@
                 state = mm_fine(mbuf[q, :64], state) + jnp.concatenate(
                     [eye if r == q else none for r in range(NB)] + [none], axis=1
                 )
+        tsend[...] = d_all[NB * FACE :]
+        for ahead in range(1, blocks_along):
+            pl.when(later(ahead))(lambda: turn_copy(ahead).start())
         starts = jnp.concatenate([mbuf[q, 64:] for q in range(NB)], axis=0)
         local[...] = mm(m_all[...], twice(starts))
+        send_rest(0)
         pl.when(jnp.logical_not(has_up))(lambda: owner_finish(0, False))
 
     for side in range(2):
@@ -376,7 +429,11 @@
 
     @pl.when(is_owner)
     def _():
-        pl.when(has_up)(lambda: owner_finish(0, False))
+        @pl.when(has_up)
+        def _():
+            form_chain()
+            owner_finish(0, False)
+
         for q in range(NB):
             pl.when(jnp.logical_not(both(owned == s, m == q)))(lambda: a_copy(q).wait_recv())
 
@@ -392,6 +449,7 @@
             coming = jnp.concatenate([obuf[k, 0, q], obuf[k, 1, q]], axis=0)
             offsets.append((known + mm(abuf[q], coming)).astype(BF16))
         local[...] = mm(m_all[...], twice(jnp.concatenate(offsets, axis=0)))
+        send_rest(k + 1)
 
     def member_gather(k):
         for side in range(2):
@@ -477,11 +535,14 @@
 
     @pl.when(is_owner)
     def _():
-        @pl.when(has_down)
-        def _():
-            @pl.loop(0, SWEEPS)
-            def _(k):
-                carry_copy(k).wait_send()
+        for ahead in range(1, blocks_along):
+            @pl.when(later(ahead))
+            def _():
+                turn_copy(ahead).wait_send()
+
+                @pl.loop(0, SWEEPS)
+                def _(k):
+                    rest_copy(k, ahead).wait_send()
 
         for q in range(NB):
             pl.when(jnp.logical_not(both(owned == s, m == q)))(lambda: last_copy(q).wait_send())
@@ -495,6 +556,7 @@
     dma = pltpu.SemaphoreType.DMA
     hbm = pl.BlockSpec(memory_space=pltpu.HBM)
     trips = SWEEPS - 1
+    before = blocks_along - 1
     placed = pl.pallas_call(
         lambda *refs: kernel(blocks_along, spans, *refs),
         name="sweeps",
@@ -537,8 +599,12 @@
             vmem((SWEEPS, NB, FACE, RHS), BF16),
             vmem((trips, 2, NB, FACE, RHS), BF16),
             vmem((trips, 2, FACE, RHS), BF16),
+            vmem((SWEEPS, before, FACE, RHS), BF16),
             vmem((SWEEPS, FACE, RHS), BF16),
-            vmem((SWEEPS, FACE, RHS), BF16),
+            vmem((before, FACE, 128), BF16),
+            vmem((FACE, 128), BF16),
+            vmem((FACE, 2 * before * FACE), BF16),
+            vmem((FACE, 128), BF16),
             vmem((FACE, RHS), BF16),
             dma((EL, 3)),
             dma((EL,)),
@@ -556,8 +622,10 @@
             dma((trips, 2)),
             dma((trips, 2)),
             dma((trips, 2)),
-            dma((SWEEPS,)),
-            dma((SWEEPS,)),
+            dma((SWEEPS, before)),
+            dma((SWEEPS, before)),
+            dma((before,)),
+            dma((before,)),
             dma((NB,)),
             dma,
         ],

time: 80.2 us -> 73.7 us (0.919)
  the two profiles are of different devices: /device:TPU:61 before, /device:TPU:59 now
where the time goes in v2:
time: 73.7 us; the launch traced here: 73.5 us
  Pallas kernels  71.6 us (97%)
  local copies, waits for them, and re-layouts  1.87 us (3%)
    pallas_call x1, Pallas kernels, shards(): pl.pallas_call(lambda *refs: kernel(blocks_along, spans, *refs), name='sw...  71.6 us
    unnamed x1, local copies, waits for them, and re-layouts  1.87 us

profile of v2, /device:TPU:59, one launch (start us, length us, event | category | flops | bytes accessed | tf_op | source)
XLA Modules:
  0.0 73.5 jit_solution(11258579350467187278)
XLA Ops:
  0.0 71.6 %sweeps.1 = bf16[4,512,128]{2,1,0:T(8,128)(2,1)} custom-call(s32[4]{0:T(128)} %bitcast.9, bf16[4,512,128]{2,1,0:T(8,128)(2,1)} %bitcast.8, bf16[4,512,512]{2,1,0:T(8,128)(2,1)} %bitcast.6, bf16[4,192,512]{2,1,0:T(8,128)(2,1)} %bitcast.7), custom_call_target="tpu_custom_call" | custom-call | tf_op jit(solution)/shard_map/sweeps/pallas_call | solution.py:560
  71.6 1.9 %copy.6 = bf16[1,1,4,512,128]{4,3,2,1,0:T(8,128)(2,1)} copy(bf16[1,1,4,512,128]{4,3,2,1,0:T(8,128)(2,1)} %bitcast.5) | data formatting | bytes 1048576

commit v3 on v2

--- a/solution.py
+++ b/solution.py
@@ -467,16 +467,17 @@
     @pl.loop(0, SWEEPS - 2)
     def _(k):
         now = member_gather(k)
+        ahead = (mm(pf_mat[:128], now) + pf_const[:128]).astype(BF16)
+        for side in range(2):
+            psend[k + 1, side] = ahead[64 * side : 64 * side + 64]
+            p_start(k + 1, side)
         for side in range(2):
             at = 128 + side * EL * FACE
             ahead = (mm(pf_mat[at : at + 256], now) + pf_const[at : at + 256]).astype(BF16)
             for p in range(EL):
                 ysend[k + 1, side, p] = ahead[p * FACE : p * FACE + FACE]
             pl.when(has_side[side])(lambda: face_copy(k + 1, side).start())
-        ahead = (mm(pf_mat[:128], now) + pf_const[:128]).astype(BF16)
-        for side in range(2):
-            psend[k + 1, side] = ahead[64 * side : 64 * side + 64]
-            p_start(k + 1, side)
+
         @pl.when(is_owner)
         def _():
             owner_gather(k)

time: 73.7 us -> 73.5 us (level)
  no operation moved by 1% of the time
where the time goes in v3:
time: 73.5 us; the launch traced here: 73.3 us
  Pallas kernels  71.4 us (97%)
  local copies, waits for them, and re-layouts  1.87 us (3%)
    pallas_call x1, Pallas kernels, shards(): pl.pallas_call(lambda *refs: kernel(blocks_along, spans, *refs), name='sw...  71.4 us
    unnamed x1, local copies, waits for them, and re-layouts  1.87 us

profile of v3, /device:TPU:59, one launch (start us, length us, event | category | flops | bytes accessed | tf_op | source)
XLA Modules:
  0.0 73.3 jit_solution(4624686229308030922)
XLA Ops:
  0.0 71.4 %sweeps.1 = bf16[4,512,128]{2,1,0:T(8,128)(2,1)} custom-call(s32[4]{0:T(128)} %bitcast.9, bf16[4,512,128]{2,1,0:T(8,128)(2,1)} %bitcast.8, bf16[4,512,512]{2,1,0:T(8,128)(2,1)} %bitcast.6, bf16[4,192,512]{2,1,0:T(8,128)(2,1)} %bitcast.7), custom_call_target="tpu_custom_call" | custom-call | tf_op jit(solution)/shard_map/sweeps/pallas_call | solution.py:561
  71.4 1.9 %copy.6 = bf16[1,1,4,512,128]{4,3,2,1,0:T(8,128)(2,1)} copy(bf16[1,1,4,512,128]{4,3,2,1,0:T(8,128)(2,1)} %bitcast.5) | data formatting | bytes 1048576
